TPU v7x, 32 devices: a whole 2x2x4 slice. The times are simulated.
32 devices in a mesh: ctx: 8 (over z, y), ch: 4 (over x, core).
Axes of the slice: x: 2, y: 2, z: 4, core: 2. Of those that a mesh axis runs over, the one named last changes fastest.
Arguments:
- tokens: bfloat16 [2048, 4096], P('ctx', 'ch'), may hold values from -6 to 6
- in_weight: bfloat16 [3, 4096, 4096], P(None, 'ctx', 'ch'), may hold values from -0.09375 to 0.09375
- short_taps: float32 [3, 3, 4096], P(None, None, 'ch'), may hold values from -4 to 4
- long_filter: float32 [4, 1024, 2048], P('ch', 'ctx'), may hold values from -0.125 to 0.125
- skip_gain: float32 [4, 1024], P('ch', 'ctx'), may hold values from 0.25 to 2
Outputs:
- gated_output: bfloat16 [4096, 2048], P('ch', 'ctx')
All inputs are finite; a program needn't handle non-finite values.
Results may differ from a plain program's by a relative error of at most 0.015.
Values may be sent and summed in bfloat16 or wider, within the bound.
A program may use at most 128 MiB of HBM per device.

v0:
```python
import math

import jax
import jax.numpy as jnp
from jax import lax
from jax.sharding import PartitionSpec as P

BLOCK = 1024


def shifted(block, axis, distance):
    devices = range(lax.axis_size(axis))
    route = [(i - distance, i) for i in devices if i - distance in devices]
    return lax.ppermute(block, axis, route)


def spectral_tables(tile_extent):
    period = 2 * tile_extent
    rows_in = jnp.arange(tile_extent, dtype=jnp.int32)[:, None]
    freq_index = jnp.arange(tile_extent, dtype=jnp.int32)
    first_slot = freq_index == 0
    phases = 2.0 * math.pi / period * (rows_in * freq_index[None, :] % period).astype(jnp.float32)
    top_phase = 2.0 * math.pi / period * (rows_in * tile_extent % period).astype(jnp.float32)
    forward_cos = jnp.cos(phases)
    forward_sin = jnp.where(first_slot[None, :], jnp.cos(top_phase), -jnp.sin(phases))
    times_out = jnp.arange(period, dtype=jnp.int32)[None, :]
    back_phases = (
        2.0 * math.pi / period * (freq_index[:, None] * times_out % period).astype(jnp.float32)
    )
    top_back = 2.0 * math.pi / period * (times_out * tile_extent % period).astype(jnp.float32)
    weights = jnp.where(first_slot, jnp.float32(1.0), jnp.float32(2.0)) / period
    inverse_cos = weights[:, None] * jnp.cos(back_phases)
    inverse_sin = jnp.where(
        first_slot[:, None], jnp.cos(top_back) / period, -(2.0 / period) * jnp.sin(back_phases)
    )
    return (forward_cos, forward_sin, inverse_cos, inverse_sin)


def global_causal_smear(gate_wave, kernel_table_lines, leftover_lines, tile_extent):
    lane_total, context_extent = gate_wave.shape
    tile_sequence_group = context_extent // tile_extent
    forward_cos, forward_sin, inverse_cos, inverse_sin = spectral_tables(tile_extent)
    first_slot = (jnp.arange(tile_extent, dtype=jnp.int32) == 0)[None, None, :]
    highest = lax.Precision.HIGHEST
    gate_wave_wide = gate_wave.astype(jnp.float32)
    source_wave = gate_wave_wide.reshape(lane_total, tile_sequence_group, tile_extent)
    kernel = kernel_table_lines.reshape(lane_total, tile_sequence_group, tile_extent)
    signal_real = jnp.einsum("cnb,bf->cnf", source_wave, forward_cos, precision=highest)
    signal_imag = jnp.einsum("cnb,bf->cnf", source_wave, forward_sin, precision=highest)
    kernel_real = jnp.einsum("cnb,bf->cnf", kernel, forward_cos, precision=highest)
    kernel_imag = jnp.einsum("cnb,bf->cnf", kernel, forward_sin, precision=highest)
    zeros_pad = jnp.zeros((lane_total, tile_sequence_group, tile_extent), jnp.float32)
    padded_real = jnp.concatenate([zeros_pad, signal_real], axis=1)
    padded_imag = jnp.concatenate([zeros_pad, signal_imag], axis=1)

    def accumulate(offset, totals):
        total_real, total_imag = totals
        shifted_real = lax.dynamic_slice_in_dim(
            padded_real, tile_sequence_group - offset, tile_sequence_group, 1
        )
        shifted_imag = lax.dynamic_slice_in_dim(
            padded_imag, tile_sequence_group - offset, tile_sequence_group, 1
        )
        filter_real = lax.dynamic_slice_in_dim(kernel_real, offset, 1, 1)
        filter_imag = lax.dynamic_slice_in_dim(kernel_imag, offset, 1, 1)
        cross = filter_imag * shifted_imag
        next_real = (
            total_real + filter_real * shifted_real - jnp.where(first_slot, jnp.float32(0.0), cross)
        )
        next_imag = total_imag + jnp.where(
            first_slot, cross, filter_real * shifted_imag + filter_imag * shifted_real
        )
        return (next_real, next_imag)

    total_real, total_imag = lax.fori_loop(
        0, tile_sequence_group, accumulate, (zeros_pad, zeros_pad)
    )
    inverse_rows = jnp.einsum("cnf,ft->cnt", total_real, inverse_cos, precision=highest)
    inverse_rows = inverse_rows + jnp.einsum(
        "cnf,ft->cnt", total_imag, inverse_sin, precision=highest
    )
    front_half = inverse_rows[:, :, :tile_extent]
    back_half = inverse_rows[:, :, tile_extent:]
    carried = jnp.concatenate(
        [jnp.zeros((lane_total, 1, tile_extent), jnp.float32), back_half[:, :-1]], axis=1
    )
    affine_mapping = (front_half + carried).reshape(lane_total, context_extent)
    return (affine_mapping + leftover_lines[:, None] * gate_wave_wide).astype(jnp.bfloat16)


def short_conv(projected_float, local_taps, previous):
    context_extent = projected_float.shape[2]
    extended = jnp.concatenate([previous, projected_float], axis=2)
    result = jnp.zeros_like(projected_float)
    for offset in range(3):
        result = (
            result
            + local_taps[:, offset, :][:, :, None]
            * extended[:, :, 2 - offset : 2 - offset + context_extent]
        )
    return result


def shards(tokens, in_weight, short_taps, long_filter, skip_gain):
    whole_tokens = lax.all_gather(tokens, "ch", axis=1, tiled=True)
    local_tokens = whole_tokens.shape[0]
    summed = jnp.einsum(
        "pdc,ld->pcl",
        lax.all_gather(in_weight, "ctx", axis=1, tiled=True),
        whole_tokens,
        preferred_element_type=jnp.float32,
    )
    projected = summed.astype(jnp.bfloat16)
    kernel_table_lines = long_filter[0]
    leftover_lines = skip_gain[0]
    last_rows = projected[:, :, local_tokens - 2 :]
    previous = shifted(last_rows, "ctx", 1)
    embedding_result = short_conv(
        projected.astype(jnp.float32), short_taps, previous.astype(jnp.float32)
    )
    gate_wave = (embedding_result[1] * embedding_result[2]).astype(jnp.bfloat16)
    per_channel_view = lax.all_to_all(gate_wave, "ctx", split_axis=0, concat_axis=1, tiled=True)
    blended_lines = global_causal_smear(per_channel_view, kernel_table_lines, leftover_lines, BLOCK)
    by_token = lax.all_to_all(blended_lines, "ctx", split_axis=1, concat_axis=0, tiled=True)
    gated_output = (embedding_result[0] * by_token.astype(jnp.float32)).astype(jnp.bfloat16)
    return gated_output


def solution(mesh):
    placed = (
        P("ctx", "ch"),
        P(None, "ctx", "ch"),
        P(None, None, "ch"),
        P("ch", "ctx", None),
        P("ch", "ctx"),
    )
    return jax.shard_map(
        shards, mesh=mesh, in_specs=placed, out_specs=P("ch", "ctx"), check_vma=False
    )
```

profile of v0, /device:TPU:28, one launch (start us, length us, event | category | flops | bytes accessed | tf_op | source)
XLA Modules:
  0.0 678.5 jit_solution(7543963728122364336)
XLA Ops:
  6.5 0.0 copy-start.6
  6.5 0.0 copy-start.7
  6.5 0.0 all-gather.5.cloned.1.call-start
  6.5 0.7 all-gather.5.cloned.1.call-update
  7.3 0.0 all-gather.3.cloned.1.call-start
  7.3 0.7 all-gather.3.cloned.1.call-update
  8.0 0.0 copy-done.6
  8.0 0.9 reshape_squeeze.3
  8.9 0.1 fusion.84
  9.0 0.1 fusion.77
  9.0 0.0 copy-done.7
  9.1 22.9 %fusion.60 = f32[128,2,1024]{0,2,1:T(8,128)} fusion(f32[128,2,1024]{2,1,0:T(2,128)S(1)} %reshape_squeeze.3), kind=kOutput, calls=%fused_computation.67 | convolution fusion | flops 3235905536 | bytes 2097152 | tf_op jit(solution)/shard_map/cnb,bf->cnf/dot_general | solution.py:50
  32.0 24.1 %fusion.63 = f32[128,2,1024]{0,2,1:T(8,128)} fusion(f32[1024]{0:T(1024)S(1)} %fusion.84, pred[1024]{0:T(1024)(128)(4,1)S(1)} %iota_compare_fusion, f32[128,2,1024]{2,1,0:T(2,128)S(1)} %reshape_squeeze.3), kind=kOutput, calls=%fused_computation.68 | convolution fusion | flops 3238002688 | bytes 2102272 | tf_op jit(solution)/shard_map/cnb,bf->cnf/dot_general | solution.py:51
  56.2 32.6 %fusion.124 = f32[1024,2048,1]{1,0,2:T(8,128)} fusion(f32[2048]{0:T(1024)S(1)} %fusion.77, pred[1024]{0:T(1024)(128)(4,1)S(1)} %iota_compare_fusion), kind=kLoop, calls=%fused_computation.17.clone.1 | loop fusion | flops 33554432 | bytes 8397824 | tf_op jit(solution)/shard_map/cnf,ft->cnt/dot_general | solution.py:79
  88.8 0.0 all-gather.5.cloned.1.call-done
  88.8 424.5 %all-gather.3.cloned.1.call-done = bf16[3,4096,1024]{2,1,0:T(8,128)(2,1)} async-done(((bf16[3,512,1024]{2,1,0:T(8,128)(2,1)}), bf16[3,4096,1024]{2,1,0:T(8,128)(2,1)}) %all-gather.3.cloned.1.call-update) | async-done | bytes 25165840 | tf_op jit(solution)/shard_map/all_gather | solution.py:109
  513.3 12.2 %fusion.114 = (f32[3,1024,256]{1,2,0:T(8,128)S(1)}, bf16[3,1024,256]{1,2,0:T(8,128)(2,1)S(1)}) fusion(bf16[3,4096,1024]{2,1,0:T(8,128)(2,1)} %all-gather.3.cloned.1.call-done, bf16[256,4096]{1,0:T(8,128)(2,1)} %all-gather.5.cloned.1.call-done), kind=kOutput, calls=%fused_computation.134 | convolution fusion | flops 6444023808 | bytes 31981568 | tf_op jit(solution)/shard_map/pdc,ld->pcl/dot_general | solution.py:107
  525.5 1.3 collective-permute-start
  526.9 4.2 collective-permute-done
  531.1 0.9 fusion.41
  532.1 0.0 copy-start.1
  532.1 1.7 copy-done.1
  533.8 0.2 fusion.72
  533.9 0.1 copy.47
  534.0 0.9 copy.19
  534.9 7.1 %all-to-all-start = ((bf16[8,128,256]{1,2,0:T(8,128)(2,1)}), bf16[8,128,256]{1,2,0:T(8,128)(2,1)S(1)}, u32[]{:S(2)}, u32[]{:S(2)}) async-start(bf16[8,128,256]{1,2,0:T(8,128)(2,1)} %copy.19), calls=%async_computation | async-start | bytes 1048576 | tf_op jit(solution)/shard_map/all_to_all | solution.py:122
  542.1 31.6 %fusion.126 = f32[1024,2048,1]{1,0,2:T(8,128)} fusion(f32[1024]{0:T(1024)S(1)} %select_multiply_fusion), kind=kLoop, calls=%fused_computation.19.clone.clone.clone.1 | loop fusion | flops 31457280 | bytes 8392704 | tf_op jit(solution)/shard_map/cnf,ft->cnt/dot_general | solution.py:78
  573.7 0.0 all-to-all-done
  573.7 0.0 copy-start.4
  573.7 20.6 %fusion.25 = f32[128,4,1024]{2,0,1:T(8,128)} fusion(bf16[128,2,1024]{0,2,1:T(8,128)(2,1)S(1)} %bitcast.86), kind=kOutput, calls=%fused_computation.38 | convolution fusion | flops 3235905536 | bytes 2621440 | tf_op jit(solution)/shard_map/concatenate | solution.py:53
  594.4 0.0 copy-done.4
  594.4 21.1 %fusion.21 = f32[128,4,1024]{2,0,1:T(8,128)} fusion(bf16[128,2,1024]{0,2,1:T(8,128)(2,1)S(1)} %bitcast.87, f32[1024]{0:T(1024)S(1)} %fusion.84, pred[1024]{0:T(1024)(128)(4,1)S(1)} %iota_compare_fusion), kind=kOutput, calls=%fused_computation.34 | convolution fusion | flops 3238002688 | bytes 2626560 | tf_op jit(solution)/shard_map/concatenate | solution.py:54
  615.5 15.7 %while.19 = (s32[]{:T(128)}, f32[128,2,1024]{2,1,0:T(2,128)}, f32[128,2,1024]{2,1,0:T(2,128)}, f32[128,2,1024]{0,2,1:T(8,128)}, f32[128,4,1024]{2,0,1:T(8,128)},...) while((s32[]{:T(128)}, f32[128,2,1024]{2,1,0:T(2,128)}, ...), condition=%wide.region_1.2_spmd.clone.clone, body=%wide.region_0.1_spmd.clone.clone.sunk | while | flops 3146759 | bytes 24119532 | solution.py:75
  615.5 0.0 copy-start.2
  615.5 0.0 copy-start.3
  615.5 1.8 constant_dynamic-slice_fusion.6
  617.4 0.0 copy-done.2
  617.4 0.3 copy-done.3
  617.7 0.1 constant_dynamic-slice_fusion.7
  617.7 1.0 copy.77
  618.7 0.2 copy.78
  618.9 4.2 select_add_fusion.3
  623.2 0.0 copy-start.2
  623.2 0.0 copy-start.3
  623.2 1.8 constant_dynamic-slice_fusion.6
  625.0 0.0 copy-done.2
  625.0 0.3 copy-done.3
  625.4 0.1 constant_dynamic-slice_fusion.7
  625.4 1.0 copy.77
  626.4 0.2 copy.78
  626.6 4.5 select_add_fusion.3
  631.1 10.4 %fusion.6 = f32[128,2,2048]{2,0,1:T(8,128)S(1)} fusion(f32[128,2,1024]{2,1,0:T(2,128)} %get-tuple-element.208, f32[1024,2048,1]{1,0,2:T(8,128)} %fusion.124), kind=kOutput, calls=%fused_computation.16 | convolution fusion | flops 6442450944 | bytes 11534336 | tf_op jit(solution)/shard_map/cnf,ft->cnt/dot_general | solution.py:79
  641.6 0.0 copy-done
  641.6 9.9 %fusion.43 = f32[128,2,2048]{2,0,1:T(8,128)S(1)} fusion(f32[128,2,2048]{2,0,1:T(8,128)S(1)} %fusion.6, f32[128,2,1024]{2,1,0:T(2,128)S(1)} %copy-done, f32[1024,2048,1]{1,0,2:T(8,128)} %fusion.126), kind=kOutput, calls=%fused_computation.58 | convolution fusion | flops 6442975232 | bytes 13631488 | tf_op jit(solution)/shard_map/cnf,ft->cnt/dot_general | solution.py:78
  651.5 0.0 copy-start.5
  651.5 0.0 copy-start.8
  651.6 0.1 slice_add_fusion
  651.7 0.3 copy.30
  652.0 0.5 copy-done.5
  652.5 0.0 copy-done.8
  652.5 0.1 add_convert_fusion
  652.7 16.4 %all_to_all.23 = bf16[128,8,256]{0,2,1:T(8,128)(2,1)S(1)} all-to-all(bf16[128,8,256]{0,2,1:T(8,128)(2,1)S(1)} %add_convert_fusion), channel_id=1, replica_groups=mesh['ctx'=8,'ch'=4] {'ctx'}, dimensions={1} | all-to-all | bytes 1048576 | tf_op jit(solution)/shard_map/all_to_all | solution.py:124
  669.1 1.3 fusion.66
  670.5 1.0 copy.32
  (13 shorter events, 0.2 us)
Async XLA Ops:
  6.5 1.5 copy-start.6
  6.5 2.5 copy-start.7
  6.5 82.2 %all-gather.5.cloned.1.call-start = ((), (), s32[]{:S(2)}) async-start(), calls=%async_computation.3 | async-start | bytes 2621440 | tf_op jit(solution)/shard_map/all_gather | solution.py:105
  7.3 506.1 %all-gather.3.cloned.1.call-start = ((), (), s32[]{:S(2)}) async-start(), calls=%async_computation.2 | async-start | bytes 28311552 | tf_op jit(solution)/shard_map/all_gather | solution.py:109
  525.5 5.6 collective-permute-start
  532.1 1.7 copy-start.1
  534.9 38.8 %all-to-all-start = ((bf16[8,128,256]{1,2,0:T(8,128)(2,1)}), bf16[8,128,256]{1,2,0:T(8,128)(2,1)S(1)}, u32[]{:S(2)}, u32[]{:S(2)}) async-start(bf16[8,128,256]{1,2,0:T(8,128)(2,1)} %copy.19), calls=%async_computation | async-start | bytes 1048576 | tf_op jit(solution)/shard_map/all_to_all | solution.py:122
  573.7 20.6 %copy-start.4 = (bf16[8,128,256]{1,2,0:T(8,128)(2,1)}, bf16[8,128,256]{1,2,0:T(8,128)(2,1)S(1)}, u32[]{:S(2)}) copy-start(bf16[8,128,256]{1,2,0:T(8,128)(2,1)S(1)} %all-to-all-done) | copy-start | bytes 1572868
  615.5 1.9 copy-start.2
  615.5 2.2 copy-start.3
  623.2 1.9 copy-start.2
  623.2 2.2 copy-start.3
  631.1 10.4 %copy-start = (f32[128,2,1024]{2,1,0:T(2,128)S(1)}, f32[128,2,1024]{2,1,0:T(2,128)}, u32[]{:S(2)}) copy-start(f32[128,2,1024]{2,1,0:T(2,128)} %get-tuple-element.207) | copy-start | bytes 3145732
  651.5 1.0 copy-start.5
  651.5 1.0 copy-start.8
Sparse Core Ops, SparseCore 0:
  8.9 23.5 all-gather.4
  34.0 479.2 all-gather.2
where the time goes:
time: 691 us; the launch traced here: 678 us
  waiting for transfers between devices  430 us (62%)
  matrix products  121 us (18%)
  other arithmetic  75.9 us (11%)
  blocking collectives  16.4 us (2%)
  between operations  13.8 us (2%)
  local copies, waits for them, and re-layouts  12.3 us (2%)
  starting transfers between devices  8.48 us (1%)
    all_gather x1, waiting for transfers between devices, shards(): lax.all_gather(in_weight, 'ctx', axis=1, tiled=True)  425 us
    dot_general x1, other arithmetic, global_causal_smear(): jnp.einsum('cnf,ft->cnt', total_imag, inverse_sin, precision=highest)  32.6 us
    dot_general x1, other arithmetic, global_causal_smear(): jnp.einsum('cnf,ft->cnt', total_real, inverse_cos, precision=highest)  31.6 us
    dot_general x1, matrix products, global_causal_smear(): jnp.einsum('cnb,bf->cnf', kernel, forward_sin, precision=highest)  24.1 us
    dot_general x1, matrix products, global_causal_smear(): jnp.einsum('cnb,bf->cnf', kernel, forward_cos, precision=highest)  22.9 us
    concatenate x1, matrix products, global_causal_smear(): padded_imag = jnp.concatenate([zeros_pad, signal_imag], axis=1)  21.1 us
    concatenate x1, matrix products, global_causal_smear(): padded_real = jnp.concatenate([zeros_pad, signal_real], axis=1)  20.6 us
    all_to_all x1, blocking collectives, shards(): lax.all_to_all(blended_lines, 'ctx', split_axis=1, concat_axis=0, tiled=T...  16.4 us
  transfers between devices with their start and end apart: 4, of which 2 were waited for; matrix products, arithmetic and copies ran while one was open for 17% of the time, Pallas kernels for 0%

commit v1 on v0

--- a/solution.py
+++ b/solution.py
@@ -2,7 +2,11 @@
 
 import jax
 import jax.numpy as jnp
+import ml_dtypes
+import numpy as np
 from jax import lax
+from jax.experimental import pallas as pl
+from jax.experimental.pallas import tpu as pltpu
 from jax.sharding import PartitionSpec as P
 
 BLOCK = 1024
@@ -126,6 +130,351 @@
     return gated_output
 
 
+NZ, NY, NX, NC = 4, 2, 2, 2
+SPECTRAL = 512
+MESH_ID = pl.DeviceIdType.MESH
+
+
+def odd_frequency_tables(tile):
+    odd = 2 * np.arange(tile, dtype=np.int64) + 1
+    turns = 2.0 * np.pi / (4 * tile)
+    times = np.arange(-tile, tile, dtype=np.int64)
+    phase = turns * ((odd[:, None] * times[None, :]) % (4 * tile))
+    forward = np.concatenate([np.cos(phase), -np.sin(phase)], axis=0)
+    back = turns * ((np.arange(tile, dtype=np.int64)[:, None] * odd[None, :]) % (4 * tile))
+    inverse = np.concatenate([np.cos(back), -np.sin(back)], axis=1) / tile
+    return forward.astype(ml_dtypes.bfloat16), inverse.astype(ml_dtypes.bfloat16)
+
+
+def mixer_kernel(
+    tokens, weight, taps, filters, skip, forward, inverse, out,
+    tok, wbuf, proj, spectrum, wave, signal, product, gate, outgoing,
+    local_sem, tok_recv, z_send, y_send, x_send, c_send, w_recv, w_send, o_recv, o_send,
+):
+    ctx_n = NZ * NY
+    rows, depth = tokens.shape
+    w_depth = weight.shape[1]
+    own = filters.shape[1]
+    tile = SPECTRAL
+    blocks = rows * ctx_n // tile
+    i, j = lax.axis_index("ctx"), lax.axis_index("ch")
+    z, y = i // NY, i % NY
+    x, c = j // NC, j % NC
+    low = z // 2
+
+    def device(zz, yy, xx, cc):
+        return (zz * NY + yy, xx * NC + cc)
+
+    def block(zz, yy, xx, cc):
+        return (zz * NY + yy) * (NX * NC) + xx * NC + cc
+
+    def push(b, sem, target):
+        return pltpu.make_async_remote_copy(
+            src_ref=tok.at[b], dst_ref=tok.at[b], send_sem=sem, recv_sem=tok_recv.at[b],
+            device_id=target, device_id_type=MESH_ID,
+        )
+
+    def up(o):
+        return push(block(o, y, x, c), z_send.at[o], device(z + 1, y, x, c))
+
+    def down(o):
+        return push(block(o, y, x, c), z_send.at[NZ + o], device(z - 1, y, x, c))
+
+    def to_y(o):
+        return push(block(o, y, x, c), y_send.at[o], device(z, 1 - y, x, c))
+
+    def to_x(o, yy):
+        return push(block(o, yy, x, c), x_send.at[o * NY + yy], device(z, y, 1 - x, c))
+
+    def to_c(o, yy, xx):
+        return push(
+            block(o, yy, xx, c), c_send.at[(o * NY + yy) * NX + xx], device(z, y, x, 1 - c)
+        )
+
+    def arrived(b):
+        pltpu.make_async_copy(tok.at[b], tok.at[b], tok_recv.at[b]).wait()
+
+    def rank(r):
+        g = r // 2
+        return (1 - g) * (z + r * (1 - 2 * (z % 2))) + g * (r + low * (3 - 2 * r))
+
+    barrier = pltpu.get_barrier_semaphore()
+    for k in range(1, ctx_n):
+        pl.semaphore_signal(
+            barrier, inc=1, device_id=((i + k) % ctx_n, j), device_id_type=MESH_ID
+        )
+    for target in (device(z, y, 1 - x, c), device(z, y, x, 1 - c)):
+        pl.semaphore_signal(barrier, inc=1, device_id=target, device_id_type=MESH_ID)
+    mine = block(z, y, x, c)
+    first = pltpu.make_async_copy(tokens, tok.at[mine], local_sem.at[0])
+    first.start()
+    own_row = pl.multiple_of(i * w_depth, w_depth)
+    own_lane = pl.multiple_of(i * own, own)
+    for p in range(3):
+        pltpu.make_async_copy(
+            weight.at[p, :, pl.ds(own_lane, own)],
+            wbuf.at[pl.ds(own_row, w_depth), pl.ds(p * own, own)],
+            local_sem.at[1],
+        ).start()
+    first.wait()
+    pl.semaphore_wait(barrier, ctx_n + 1)
+
+    @pl.when(z < NZ - 1)
+    def _():
+        up(z).start()
+
+    @pl.when(z > 0)
+    def _():
+        down(z).start()
+
+    to_y(z).start()
+    to_x(z, y).start()
+    to_c(z, y, x).start()
+
+    def weight_push(k, p):
+        peer = (i + k) % ctx_n
+        return pltpu.make_async_remote_copy(
+            src_ref=weight.at[p, :, pl.ds(pl.multiple_of(peer * own, own), own)],
+            dst_ref=wbuf.at[pl.ds(own_row, w_depth), pl.ds(p * own, own)],
+            send_sem=w_send.at[(k - 1) * 3 + p], recv_sem=w_recv.at[i],
+            device_id=(peer, j), device_id_type=MESH_ID,
+        )
+
+    for k in range(1, ctx_n):
+        for p in range(3):
+            weight_push(k, p).start()
+
+    def z_step(r):
+        o = rank(r)
+        arrived(block(o, y, x, c))
+
+        @pl.when(jnp.logical_and(o < z, z < NZ - 1))
+        def _():
+            up(o).start()
+
+        @pl.when(jnp.logical_and(o > z, z > 0))
+        def _():
+            down(o).start()
+
+        to_y(o).start()
+        to_x(o, y).start()
+        to_c(o, y, x).start()
+
+    def y_step(r):
+        o = rank(r)
+        arrived(block(o, 1 - y, x, c))
+        to_x(o, 1 - y).start()
+        to_c(o, 1 - y, x).start()
+
+    for n in range(blocks):
+        lo = max(n - 1, 0) * tile
+        window = filters[0, :, lo : (n + 1) * tile].astype(jnp.bfloat16)
+        table = forward[:, tile:] if n == 0 else forward[...]
+        spectrum[:, n * own : (n + 1) * own] = lax.dot_general(
+            table, window, (((1,), (1,)), ((), ())), preferred_element_type=jnp.float32
+        )
+
+    z_step(1)
+    y_step(0)
+    z_step(2)
+    y_step(1)
+    z_step(3)
+    y_step(2)
+    y_step(3)
+
+    proj[0:8, :] = jnp.zeros((8, 3 * own), jnp.float32)
+
+    def project(s):
+        o, yy = rank(s // 2), (y + s) % 2
+        arrived(block(o, yy, x, 1 - c))
+        arrived(block(o, yy, 1 - x, 1 - c))
+        total = None
+        for q in range(NX * NC):
+            part = jnp.dot(
+                tok[(o * NY + yy) * (NX * NC) + q],
+                wbuf[q * depth : (q + 1) * depth, :],
+                preferred_element_type=jnp.float32,
+            )
+            total = part if total is None else total + part
+        row = pl.multiple_of(8 + (o * NY + yy) * rows, 8)
+        proj[pl.ds(row, rows), :] = total.astype(jnp.bfloat16).astype(jnp.float32)
+
+    def x_step(s):
+        o, yy = rank(s // 2), (y + s) % 2
+        arrived(block(o, yy, 1 - x, c))
+        to_c(o, yy, 1 - x).start()
+
+    lead = 4
+    for s in range(lead):
+        x_step(s)
+    whole_row = wbuf.at[pl.ds(own_row, w_depth), :]
+    pltpu.make_async_copy(whole_row, whole_row, local_sem.at[1]).wait()
+    for k in range(1, ctx_n):
+        peer = (i + k) % ctx_n
+        piece = wbuf.at[pl.ds(pl.multiple_of(peer * w_depth, w_depth), w_depth), :]
+        pltpu.make_async_copy(piece, piece, w_recv.at[peer]).wait()
+
+    @pl.loop(0, NZ * NY)
+    def _(s):
+        @pl.when(s < NZ * NY - lead)
+        def _():
+            x_step(s + lead)
+
+        project(s)
+
+    tap = [
+        [taps[p, t : t + 1, pl.ds(own_lane, own)] for t in range(3)] for p in range(3)
+    ]
+    for q in range(ctx_n):
+        start = 8 + q * rows
+        feature = []
+        for p in range(3):
+            lanes = slice(p * own, (p + 1) * own)
+            total = tap[p][0] * proj[start : start + rows, lanes]
+            total = total + tap[p][1] * proj[start - 1 : start - 1 + rows, lanes]
+            feature.append(total + tap[p][2] * proj[start - 2 : start - 2 + rows, lanes])
+        gate[q * rows : (q + 1) * rows, :] = feature[0]
+        n, at = q * rows // tile, q * rows % tile
+        wave[at : at + rows, n * own : (n + 1) * own] = (feature[1] * feature[2]).astype(
+            jnp.bfloat16
+        )
+    signal[...] = jnp.dot(forward[:, tile:], wave[...], preferred_element_type=jnp.float32)
+
+    @pl.loop(0, tile // 16)
+    def _(step):
+        re = pl.ds(pl.multiple_of(step * 16, 16), 16)
+        im = pl.ds(pl.multiple_of(tile + step * 16, 16), 16)
+        lanes = [pl.ds(n * own, own) for n in range(blocks)]
+        kr, ki = [spectrum[re, a] for a in lanes], [spectrum[im, a] for a in lanes]
+        sr, si = [signal[re, a] for a in lanes], [signal[im, a] for a in lanes]
+        for n in range(blocks):
+            real, imag = 0.0, 0.0
+            for m in range(n + 1):
+                real = real + (kr[n - m] * sr[m] - ki[n - m] * si[m])
+                imag = imag + (kr[n - m] * si[m] + ki[n - m] * sr[m])
+            product[re, lanes[n]] = real.astype(jnp.bfloat16)
+            product[im, lanes[n]] = imag.astype(jnp.bfloat16)
+
+    def out_push(q):
+        return pltpu.make_async_remote_copy(
+            src_ref=outgoing.at[q], dst_ref=out.at[pl.ds(own_lane, own), :],
+            send_sem=o_send.at[q], recv_sem=o_recv.at[i],
+            device_id=(q, j), device_id_type=MESH_ID,
+        )
+
+    def out_keep(q):
+        return pltpu.make_async_copy(
+            outgoing.at[q], out.at[pl.ds(own_lane, own), :], o_send.at[q]
+        )
+
+    gain = skip[...]
+    for n in range(blocks):
+        lanes = slice(n * own, (n + 1) * own)
+        smeared = jnp.dot(inverse[...], product[:, lanes], preferred_element_type=jnp.float32)
+        for half in range(tile // rows):
+            q = n * (tile // rows) + half
+            at = slice(half * rows, (half + 1) * rows)
+            mixed = smeared[at] + gain * wave[at, lanes].astype(jnp.float32)
+            mixed = mixed.astype(jnp.bfloat16).astype(jnp.float32)
+            gated = gate[q * rows : (q + 1) * rows, :] * mixed
+            outgoing[q] = gated.T.astype(jnp.bfloat16)
+
+            @pl.when(i != q)
+            def _():
+                out_push(q).start()
+
+            @pl.when(i == q)
+            def _():
+                out_keep(q).start()
+
+    for o in range(NZ):
+        @pl.when(jnp.logical_and(o <= z, z < NZ - 1))
+        def _():
+            up(o).wait_send()
+
+        @pl.when(jnp.logical_and(o >= z, z > 0))
+        def _():
+            down(o).wait_send()
+
+        to_y(o).wait_send()
+        for yy in range(NY):
+            to_x(o, yy).wait_send()
+            for xx in range(NX):
+                to_c(o, yy, xx).wait_send()
+    for k in range(1, ctx_n):
+        for p in range(3):
+            weight_push(k, p).wait_send()
+    for q in range(ctx_n):
+        @pl.when(i != q)
+        def _():
+            out_push(q).wait_send()
+            landed = out.at[pl.ds(q * own, own), :]
+            pltpu.make_async_copy(landed, landed, o_recv.at[q]).wait()
+
+        @pl.when(i == q)
+        def _():
+            out_keep(q).wait()
+
+
+def fused_shards(tokens, in_weight, short_taps, long_filter, skip_gain):
+    rows, depth = tokens.shape
+    ctx_n, ch_n = NZ * NY, NX * NC
+    own = long_filter.shape[1]
+    span = rows * ctx_n
+    tile = SPECTRAL
+    lanes = span // tile * own
+    forward, inverse = odd_frequency_tables(tile)
+    vmem = pl.BlockSpec(memory_space=pltpu.VMEM)
+    hbm = pl.BlockSpec(memory_space=pl.ANY)
+    dma = pltpu.SemaphoreType.DMA
+    flops = 2 * span * depth * ch_n * 3 * own
+    return pl.pallas_call(
+        mixer_kernel,
+        out_shape=jax.ShapeDtypeStruct((ctx_n * own, rows), jnp.bfloat16),
+        in_specs=[hbm, hbm, vmem, vmem, vmem, vmem, vmem],
+        out_specs=hbm,
+        scratch_shapes=[
+            pltpu.VMEM((ctx_n * ch_n, rows, depth), jnp.bfloat16),
+            pltpu.VMEM((depth * ch_n, 3 * own), jnp.bfloat16),
+            pltpu.VMEM((8 + span, 3 * own), jnp.float32),
+            pltpu.VMEM((2 * tile, lanes), jnp.float32),
+            pltpu.VMEM((tile, lanes), jnp.bfloat16),
+            pltpu.VMEM((2 * tile, lanes), jnp.float32),
+            pltpu.VMEM((2 * tile, lanes), jnp.bfloat16),
+            pltpu.VMEM((span, own), jnp.float32),
+            pltpu.VMEM((ctx_n, own, rows), jnp.bfloat16),
+            dma((2,)),
+            dma((ctx_n * ch_n,)),
+            dma((2 * NZ,)),
+            dma((NZ,)),
+            dma((ctx_n,)),
+            dma((ctx_n * NX,)),
+            dma((ctx_n,)),
+            dma((3 * (ctx_n - 1),)),
+            dma((ctx_n,)),
+            dma((ctx_n,)),
+        ],
+        compiler_params=pltpu.CompilerParams(
+            collective_id=0, has_side_effects=True, vmem_limit_bytes=56 * 1024 * 1024
+        ),
+        cost_estimate=pl.CostEstimate(
+            flops=flops, bytes_accessed=2 * tokens.size * ctx_n * ch_n, transcendentals=0
+        ),
+        name="mixer",
+    )(tokens, in_weight, short_taps, long_filter, skip_gain, jnp.asarray(forward), jnp.asarray(inverse))
+
+
+def fits(mesh, tokens, in_weight, long_filter):
+    span, depth = tokens.shape
+    return (
+        dict(mesh.shape) == {"ctx": NZ * NY, "ch": NX * NC}
+        and span == NZ * NY * 256
+        and depth == NX * NC * 1024
+        and in_weight.shape[2] == long_filter.shape[0] * long_filter.shape[1]
+        and long_filter.shape[1] == NZ * NY * 128
+    )
+
+
 def solution(mesh):
     placed = (
         P("ctx", "ch"),
@@ -134,6 +483,11 @@
         P("ch", "ctx", None),
         P("ch", "ctx"),
     )
-    return jax.shard_map(
-        shards, mesh=mesh, in_specs=placed, out_specs=P("ch", "ctx"), check_vma=False
-    )
+
+    def run(tokens, in_weight, short_taps, long_filter, skip_gain):
+        body = fused_shards if fits(mesh, tokens, in_weight, long_filter) else shards
+        return jax.shard_map(
+            body, mesh=mesh, in_specs=placed, out_specs=P("ch", "ctx"), check_vma=False
+        )(tokens, in_weight, short_taps, long_filter, skip_gain)
+
+    return run

time: 691 us -> 165 us (0.24); the launches traced: 678 us -> 164 us
  waiting for transfers between devices: 430 us -> 0 us
  Pallas kernels: 0 us -> 162 us
  matrix products: 121 us -> 0 us
  other arithmetic: 75.9 us -> 0 us
  blocking collectives: 16.4 us -> 0 us
  between operations: 13.8 us -> 0.01 us
  local copies, waits for them, and re-layouts: 12.3 us -> 1.87 us
  starting transfers between devices: 8.48 us -> 0 us
    all_gather x2 -> x0, waiting for transfers between devices: 425 us -> none  [the longest x1 425 us: shards(): lax.all_gather(in_weight, 'ctx', axis=1, tiled=True)]
    pallas_call x0 -> x1, Pallas kernels: none -> 162 us  [fused_shards(): pl.pallas_call(mixer_kernel, out_shape=jax.ShapeDtypeStruct((ctx_n * own,...]
    dot_general x5 -> x0, matrix products: 79.5 us -> none  [the longest x1 24.1 us: global_causal_smear(): jnp.einsum('cnb,bf->cnf', kernel, forward_sin, precision=highest)]
    dot_general x2 -> x0, other arithmetic: 64.3 us -> none  [the longest x1 32.6 us: global_causal_smear(): jnp.einsum('cnf,ft->cnt', total_imag, inverse_sin, precision=highest)]
    concatenate x2 -> x0, matrix products: 41.7 us -> none  [the longest x1 21.1 us: global_causal_smear(): padded_imag = jnp.concatenate([zeros_pad, signal_imag], axis=1)]
    all_to_all x1 -> x0, blocking collectives: 16.4 us -> none  [shards(): lax.all_to_all(blended_lines, 'ctx', split_axis=1, concat_axis=0, tiled=T...]
    add x4 -> x0, other arithmetic: 9.77 us -> none  [the longest x2 8.74 us: accumulate(): total_imag + jnp.where(first_slot, cross, filter_real * shifted_imag + fi...]
    all_to_all x1 -> x0, starting transfers between devices: 7.15 us -> none  [shards(): lax.all_to_all(gate_wave, 'ctx', split_axis=0, concat_axis=1, tiled=True)]
  transfers between devices with their start and end apart: 4 -> 0, of which waited for: 2 -> 0; matrix products, arithmetic and copies ran while one was open for 17% -> 0% of each run, Pallas kernels for 0% -> 0%
where the time goes in v1:
time: 165 us; the launch traced here: 164 us
  Pallas kernels  162 us (98%)
  local copies, waits for them, and re-layouts  1.87 us (1%)
    pallas_call x1, Pallas kernels, fused_shards(): pl.pallas_call(mixer_kernel, out_shape=jax.ShapeDtypeStruct((ctx_n * own,...  162 us

profile of v1, /device:TPU:28, one launch (start us, length us, event | category | flops | bytes accessed | tf_op | source)
XLA Modules:
  0.0 163.9 jit_solution(7555986233218553704)
XLA Ops:
  0.0 162.1 %mixer.1 = bf16[1024,256]{1,0:T(8,128)(2,1)} custom-call(bf16[256,1024]{1,0:T(8,128)(2,1)} %tokens.1, bf16[3,512,1024]{2,1,0:T(8,128)(2,1)} %weight.1, f32[3,3,1024]{2,1,0:T(4,128)} %taps.1, f32[1,128,2048]{2,1,0:T(8,128)} %filters.1, f32[1,128]{1,0:T(1,128)} %skip.1, bf16[1024,1024]{1,0:T(8,128)(2,1)} %constant.4.clone.forward, ...), custom_call_target="tpu_custom_call" | custom-call | flops 6442450944 | bytes 16777216 | tf_op jit(solution)/shard_map/mixer/pallas_call | solution.py:431
  162.1 1.9 %copy.9 = bf16[1024,256]{1,0:T(8,128)(2,1)} copy(bf16[1024,256]{1,0:T(8,128)(2,1)} %mixer.1) | data formatting | bytes 1048576

commit v2 on v1

--- a/solution.py
+++ b/solution.py
@@ -147,14 +147,15 @@
 
 
 def mixer_kernel(
-    tokens, weight, taps, filters, skip, forward, inverse, out,
-    tok, wbuf, proj, spectrum, wave, signal, product, gate, outgoing,
+    tokens, weight, taps, filters_in, skip, forward_in, inverse_in, out,
+    filters, forward, inverse, tok, wbuf, proj, spectrum, wave, signal, product, gate, outgoing,
     local_sem, tok_recv, z_send, y_send, x_send, c_send, w_recv, w_send, o_recv, o_send,
 ):
     ctx_n = NZ * NY
     rows, depth = tokens.shape
     w_depth = weight.shape[1]
     own = filters.shape[1]
+    staged = ((filters_in, filters), (forward_in, forward), (inverse_in, inverse))
     tile = SPECTRAL
     blocks = rows * ctx_n // tile
     i, j = lax.axis_index("ctx"), lax.axis_index("ch")
@@ -216,6 +217,8 @@
             wbuf.at[pl.ds(own_row, w_depth), pl.ds(p * own, own)],
             local_sem.at[1],
         ).start()
+    for k, (src, dst) in enumerate(staged):
+        pltpu.make_async_copy(src, dst, local_sem.at[2 + k]).start()
     first.wait()
     pl.semaphore_wait(barrier, ctx_n + 1)
 
@@ -231,18 +234,18 @@
     to_x(z, y).start()
     to_c(z, y, x).start()
 
-    def weight_push(k, p):
-        peer = (i + k) % ctx_n
+    def weight_push(peer, p):
         return pltpu.make_async_remote_copy(
             src_ref=weight.at[p, :, pl.ds(pl.multiple_of(peer * own, own), own)],
             dst_ref=wbuf.at[pl.ds(own_row, w_depth), pl.ds(p * own, own)],
-            send_sem=w_send.at[(k - 1) * 3 + p], recv_sem=w_recv.at[i],
+            send_sem=w_send.at[peer * 3 + p], recv_sem=w_recv.at[i],
             device_id=(peer, j), device_id_type=MESH_ID,
         )
 
-    for k in range(1, ctx_n):
-        for p in range(3):
-            weight_push(k, p).start()
+    def push_weights(zz, ys):
+        for yy in ys:
+            for p in range(3):
+                weight_push(zz * NY + yy, p).start()
 
     def z_step(r):
         o = rank(r)
@@ -265,6 +268,9 @@
         arrived(block(o, 1 - y, x, c))
         to_x(o, 1 - y).start()
         to_c(o, 1 - y, x).start()
+
+    for k, (src, dst) in enumerate(staged):
+        pltpu.make_async_copy(src, dst, local_sem.at[2 + k]).wait()
 
     for n in range(blocks):
         lo = max(n - 1, 0) * tile
@@ -276,7 +282,11 @@
 
     z_step(1)
     y_step(0)
+    push_weights(z, (1 - y,))
     z_step(2)
+    push_weights(rank(3), (y, 1 - y))
+    push_weights(rank(2), (y, 1 - y))
+    push_weights(rank(1), (y, 1 - y))
     y_step(1)
     z_step(3)
     y_step(2)
@@ -284,20 +294,27 @@
 
     proj[0:8, :] = jnp.zeros((8, 3 * own), jnp.float32)
 
-    def project(s):
+    def project(s, ranks, begin, end):
         o, yy = rank(s // 2), (y + s) % 2
-        arrived(block(o, yy, x, 1 - c))
-        arrived(block(o, yy, 1 - x, 1 - c))
-        total = None
-        for q in range(NX * NC):
+        row = pl.multiple_of(8 + (o * NY + yy) * rows, 8)
+        total = None if begin else proj[pl.ds(row, rows), :]
+        for r in ranks:
+            q = rank(r)
             part = jnp.dot(
                 tok[(o * NY + yy) * (NX * NC) + q],
-                wbuf[q * depth : (q + 1) * depth, :],
+                wbuf[pl.ds(pl.multiple_of(q * depth, depth), depth), :],
                 preferred_element_type=jnp.float32,
             )
             total = part if total is None else total + part
-        row = pl.multiple_of(8 + (o * NY + yy) * rows, 8)
-        proj[pl.ds(row, rows), :] = total.astype(jnp.bfloat16).astype(jnp.float32)
+        if end:
+            total = total.astype(jnp.bfloat16).astype(jnp.float32)
+        proj[pl.ds(row, rows), :] = total
+
+    def weights_from(zz, ys):
+        for yy in ys:
+            peer = zz * NY + yy
+            piece = wbuf.at[pl.ds(pl.multiple_of(peer * w_depth, w_depth), w_depth), :]
+            pltpu.make_async_copy(piece, piece, w_recv.at[peer]).wait()
 
     def x_step(s):
         o, yy = rank(s // 2), (y + s) % 2
@@ -309,10 +326,8 @@
         x_step(s)
     whole_row = wbuf.at[pl.ds(own_row, w_depth), :]
     pltpu.make_async_copy(whole_row, whole_row, local_sem.at[1]).wait()
-    for k in range(1, ctx_n):
-        peer = (i + k) % ctx_n
-        piece = wbuf.at[pl.ds(pl.multiple_of(peer * w_depth, w_depth), w_depth), :]
-        pltpu.make_async_copy(piece, piece, w_recv.at[peer]).wait()
+    weights_from(z, (1 - y,))
+    weights_from(rank(1), (y, 1 - y))
 
     @pl.loop(0, NZ * NY)
     def _(s):
@@ -320,7 +335,17 @@
         def _():
             x_step(s + lead)
 
-        project(s)
+        o, yy = rank(s // 2), (y + s) % 2
+        arrived(block(o, yy, x, 1 - c))
+        arrived(block(o, yy, 1 - x, 1 - c))
+        project(s, (0, 1), True, False)
+
+    weights_from(rank(2), (y, 1 - y))
+    weights_from(rank(3), (y, 1 - y))
+
+    @pl.loop(0, NZ * NY)
+    def _(s):
+        project(s, (2, 3), False, True)
 
     tap = [
         [taps[p, t : t + 1, pl.ds(own_lane, own)] for t in range(3)] for p in range(3)
@@ -401,12 +426,11 @@
             to_x(o, yy).wait_send()
             for xx in range(NX):
                 to_c(o, yy, xx).wait_send()
-    for k in range(1, ctx_n):
-        for p in range(3):
-            weight_push(k, p).wait_send()
     for q in range(ctx_n):
         @pl.when(i != q)
         def _():
+            for p in range(3):
+                weight_push(q, p).wait_send()
             out_push(q).wait_send()
             landed = out.at[pl.ds(q * own, own), :]
             pltpu.make_async_copy(landed, landed, o_recv.at[q]).wait()
@@ -431,9 +455,12 @@
     return pl.pallas_call(
         mixer_kernel,
         out_shape=jax.ShapeDtypeStruct((ctx_n * own, rows), jnp.bfloat16),
-        in_specs=[hbm, hbm, vmem, vmem, vmem, vmem, vmem],
+        in_specs=[hbm, hbm, vmem, hbm, vmem, hbm, hbm],
         out_specs=hbm,
         scratch_shapes=[
+            pltpu.VMEM(long_filter.shape, jnp.float32),
+            pltpu.VMEM(forward.shape, jnp.bfloat16),
+            pltpu.VMEM(inverse.shape, jnp.bfloat16),
             pltpu.VMEM((ctx_n * ch_n, rows, depth), jnp.bfloat16),
             pltpu.VMEM((depth * ch_n, 3 * own), jnp.bfloat16),
             pltpu.VMEM((8 + span, 3 * own), jnp.float32),
@@ -443,14 +470,14 @@
             pltpu.VMEM((2 * tile, lanes), jnp.bfloat16),
             pltpu.VMEM((span, own), jnp.float32),
             pltpu.VMEM((ctx_n, own, rows), jnp.bfloat16),
-            dma((2,)),
+            dma((5,)),
             dma((ctx_n * ch_n,)),
             dma((2 * NZ,)),
             dma((NZ,)),
             dma((ctx_n,)),
             dma((ctx_n * NX,)),
             dma((ctx_n,)),
-            dma((3 * (ctx_n - 1),)),
+            dma((3 * ctx_n,)),
             dma((ctx_n,)),
             dma((ctx_n,)),
         ],

time: 165 us -> 152 us (0.921)
  Pallas kernels: 162 us -> 149 us
    pallas_call x1, Pallas kernels: 162 us -> 149 us  [fused_shards(): pl.pallas_call(mixer_kernel, out_shape=jax.ShapeDtypeStruct((ctx_n * own,...]
where the time goes in v2:
time: 152 us; the launch traced here: 151 us
  Pallas kernels  149 us (98%)
  local copies, waits for them, and re-layouts  1.87 us (1%)
    pallas_call x1, Pallas kernels, fused_shards(): pl.pallas_call(mixer_kernel, out_shape=jax.ShapeDtypeStruct((ctx_n * own,...  149 us

profile of v2, /device:TPU:28, one launch (start us, length us, event | category | flops | bytes accessed | tf_op | source)
XLA Modules:
  0.0 150.8 jit_solution(2575517920983149005)
XLA Ops:
  0.0 148.9 %mixer.1 = bf16[1024,256]{1,0:T(8,128)(2,1)} custom-call(bf16[256,1024]{1,0:T(8,128)(2,1)} %tokens.1, bf16[3,512,1024]{2,1,0:T(8,128)(2,1)} %weight.1, f32[3,3,1024]{2,1,0:T(4,128)} %taps.1, f32[1,128,2048]{2,1,0:T(8,128)} %filters_in.1, f32[1,128]{1,0:T(1,128)} %skip.1, bf16[1024,1024]{1,0:T(8,128)(2,1)} %constant.4.clone.forward_in, ...), custom_call_target="tpu_custom_call" | custom-call | flops 6442450944 | bytes 16777216 | tf_op jit(solution)/shard_map/mixer/pallas_call | solution.py:455
  148.9 1.9 %copy.9 = bf16[1024,256]{1,0:T(8,128)(2,1)} copy(bf16[1024,256]{1,0:T(8,128)(2,1)} %mixer.1) | data formatting | bytes 1048576

commit v3 on v2

--- a/solution.py
+++ b/solution.py
@@ -148,7 +148,7 @@
 
 def mixer_kernel(
     tokens, weight, taps, filters_in, skip, forward_in, inverse_in, out,
-    filters, forward, inverse, tok, wbuf, proj, spectrum, wave, signal, product, gate, outgoing,
+    filters, forward, inverse, tok, wsend, wbuf, proj, spectrum, wave, signal, product, gate, outgoing,
     local_sem, tok_recv, z_send, y_send, x_send, c_send, w_recv, w_send, o_recv, o_send,
 ):
     ctx_n = NZ * NY
@@ -211,12 +211,13 @@
     first.start()
     own_row = pl.multiple_of(i * w_depth, w_depth)
     own_lane = pl.multiple_of(i * own, own)
-    for p in range(3):
-        pltpu.make_async_copy(
-            weight.at[p, :, pl.ds(own_lane, own)],
-            wbuf.at[pl.ds(own_row, w_depth), pl.ds(p * own, own)],
-            local_sem.at[1],
-        ).start()
+    for peer in range(ctx_n):
+        for p in range(3):
+            pltpu.make_async_copy(
+                weight.at[p, :, pl.ds(peer * own, own)],
+                wsend.at[peer, :, pl.ds(p * own, own)],
+                local_sem.at[1],
+            ).start()
     for k, (src, dst) in enumerate(staged):
         pltpu.make_async_copy(src, dst, local_sem.at[2 + k]).start()
     first.wait()
@@ -234,18 +235,16 @@
     to_x(z, y).start()
     to_c(z, y, x).start()
 
-    def weight_push(peer, p):
+    def weight_push(peer):
         return pltpu.make_async_remote_copy(
-            src_ref=weight.at[p, :, pl.ds(pl.multiple_of(peer * own, own), own)],
-            dst_ref=wbuf.at[pl.ds(own_row, w_depth), pl.ds(p * own, own)],
-            send_sem=w_send.at[peer * 3 + p], recv_sem=w_recv.at[i],
+            src_ref=wsend.at[peer], dst_ref=wbuf.at[pl.ds(own_row, w_depth), :],
+            send_sem=w_send.at[peer], recv_sem=w_recv.at[i],
             device_id=(peer, j), device_id_type=MESH_ID,
         )
 
     def push_weights(zz, ys):
         for yy in ys:
-            for p in range(3):
-                weight_push(zz * NY + yy, p).start()
+            weight_push(zz * NY + yy).start()
 
     def z_step(r):
         o = rank(r)
@@ -280,28 +279,33 @@
             table, window, (((1,), (1,)), ((), ())), preferred_element_type=jnp.float32
         )
 
+    pltpu.make_async_copy(wsend, wsend, local_sem.at[1]).wait()
+    own_weights = pltpu.make_async_copy(
+        wsend.at[i], wbuf.at[pl.ds(own_row, w_depth), :], local_sem.at[5]
+    )
+    own_weights.start()
+
     z_step(1)
     y_step(0)
     push_weights(z, (1 - y,))
     z_step(2)
     push_weights(rank(3), (y, 1 - y))
-    push_weights(rank(2), (y, 1 - y))
-    push_weights(rank(1), (y, 1 - y))
     y_step(1)
     z_step(3)
+    push_weights(rank(2), (y, 1 - y))
     y_step(2)
+    push_weights(rank(1), (y, 1 - y))
     y_step(3)
 
     proj[0:8, :] = jnp.zeros((8, 3 * own), jnp.float32)
 
-    def project(s, ranks, begin, end):
-        o, yy = rank(s // 2), (y + s) % 2
-        row = pl.multiple_of(8 + (o * NY + yy) * rows, 8)
+    def project(at, ranks, begin, end):
+        row = 8 + at * rows if isinstance(at, int) else pl.multiple_of(8 + at * rows, 8)
         total = None if begin else proj[pl.ds(row, rows), :]
         for r in ranks:
             q = rank(r)
             part = jnp.dot(
-                tok[(o * NY + yy) * (NX * NC) + q],
+                tok[at * (NX * NC) + q],
                 wbuf[pl.ds(pl.multiple_of(q * depth, depth), depth), :],
                 preferred_element_type=jnp.float32,
             )
@@ -324,8 +328,7 @@
     lead = 4
     for s in range(lead):
         x_step(s)
-    whole_row = wbuf.at[pl.ds(own_row, w_depth), :]
-    pltpu.make_async_copy(whole_row, whole_row, local_sem.at[1]).wait()
+    own_weights.wait()
     weights_from(z, (1 - y,))
     weights_from(rank(1), (y, 1 - y))
 
@@ -338,19 +341,17 @@
         o, yy = rank(s // 2), (y + s) % 2
         arrived(block(o, yy, x, 1 - c))
         arrived(block(o, yy, 1 - x, 1 - c))
-        project(s, (0, 1), True, False)
+        project(o * NY + yy, (0, 1), True, False)
 
     weights_from(rank(2), (y, 1 - y))
     weights_from(rank(3), (y, 1 - y))
-
-    @pl.loop(0, NZ * NY)
-    def _(s):
-        project(s, (2, 3), False, True)
 
     tap = [
         [taps[p, t : t + 1, pl.ds(own_lane, own)] for t in range(3)] for p in range(3)
     ]
-    for q in range(ctx_n):
+    gain = skip[...]
+
+    def features(q):
         start = 8 + q * rows
         feature = []
         for p in range(3):
@@ -363,22 +364,22 @@
         wave[at : at + rows, n * own : (n + 1) * own] = (feature[1] * feature[2]).astype(
             jnp.bfloat16
         )
-    signal[...] = jnp.dot(forward[:, tile:], wave[...], preferred_element_type=jnp.float32)
-
-    @pl.loop(0, tile // 16)
-    def _(step):
-        re = pl.ds(pl.multiple_of(step * 16, 16), 16)
-        im = pl.ds(pl.multiple_of(tile + step * 16, 16), 16)
-        lanes = [pl.ds(n * own, own) for n in range(blocks)]
-        kr, ki = [spectrum[re, a] for a in lanes], [spectrum[im, a] for a in lanes]
-        sr, si = [signal[re, a] for a in lanes], [signal[im, a] for a in lanes]
-        for n in range(blocks):
+
+    def multiply(n):
+        lanes = [pl.ds(m * own, own) for m in range(n + 1)]
+
+        @pl.loop(0, tile // 16, unroll=4)
+        def _(step):
+            re = pl.ds(pl.multiple_of(step * 16, 16), 16)
+            im = pl.ds(pl.multiple_of(tile + step * 16, 16), 16)
             real, imag = 0.0, 0.0
             for m in range(n + 1):
-                real = real + (kr[n - m] * sr[m] - ki[n - m] * si[m])
-                imag = imag + (kr[n - m] * si[m] + ki[n - m] * sr[m])
-            product[re, lanes[n]] = real.astype(jnp.bfloat16)
-            product[im, lanes[n]] = imag.astype(jnp.bfloat16)
+                kr, ki = spectrum[re, lanes[n - m]], spectrum[im, lanes[n - m]]
+                sr, si = signal[re, lanes[m]], signal[im, lanes[m]]
+                real = real + (kr * sr - ki * si)
+                imag = imag + (kr * si + ki * sr)
+            product[re, :] = real.astype(jnp.bfloat16)
+            product[im, :] = imag.astype(jnp.bfloat16)
 
     def out_push(q):
         return pltpu.make_async_remote_copy(
@@ -392,12 +393,19 @@
             outgoing.at[q], out.at[pl.ds(own_lane, own), :], o_send.at[q]
         )
 
-    gain = skip[...]
+    per_tile = tile // rows
     for n in range(blocks):
         lanes = slice(n * own, (n + 1) * own)
-        smeared = jnp.dot(inverse[...], product[:, lanes], preferred_element_type=jnp.float32)
-        for half in range(tile // rows):
-            q = n * (tile // rows) + half
+        for half in range(per_tile):
+            project(n * per_tile + half, (2, 3), False, True)
+            features(n * per_tile + half)
+        signal[:, lanes] = jnp.dot(
+            forward[:, tile:], wave[:, lanes], preferred_element_type=jnp.float32
+        )
+        multiply(n)
+        smeared = jnp.dot(inverse[...], product[...], preferred_element_type=jnp.float32)
+        for half in range(per_tile):
+            q = n * per_tile + half
             at = slice(half * rows, (half + 1) * rows)
             mixed = smeared[at] + gain * wave[at, lanes].astype(jnp.float32)
             mixed = mixed.astype(jnp.bfloat16).astype(jnp.float32)
@@ -429,8 +437,7 @@
     for q in range(ctx_n):
         @pl.when(i != q)
         def _():
-            for p in range(3):
-                weight_push(q, p).wait_send()
+            weight_push(q).wait_send()
             out_push(q).wait_send()
             landed = out.at[pl.ds(q * own, own), :]
             pltpu.make_async_copy(landed, landed, o_recv.at[q]).wait()
@@ -462,22 +469,23 @@
             pltpu.VMEM(forward.shape, jnp.bfloat16),
             pltpu.VMEM(inverse.shape, jnp.bfloat16),
             pltpu.VMEM((ctx_n * ch_n, rows, depth), jnp.bfloat16),
+            pltpu.VMEM((ctx_n, in_weight.shape[1], 3 * own), jnp.bfloat16),
             pltpu.VMEM((depth * ch_n, 3 * own), jnp.bfloat16),
             pltpu.VMEM((8 + span, 3 * own), jnp.float32),
             pltpu.VMEM((2 * tile, lanes), jnp.float32),
             pltpu.VMEM((tile, lanes), jnp.bfloat16),
             pltpu.VMEM((2 * tile, lanes), jnp.float32),
-            pltpu.VMEM((2 * tile, lanes), jnp.bfloat16),
+            pltpu.VMEM((2 * tile, own), jnp.bfloat16),
             pltpu.VMEM((span, own), jnp.float32),
             pltpu.VMEM((ctx_n, own, rows), jnp.bfloat16),
-            dma((5,)),
+            dma((6,)),
             dma((ctx_n * ch_n,)),
             dma((2 * NZ,)),
             dma((NZ,)),
             dma((ctx_n,)),
             dma((ctx_n * NX,)),
             dma((ctx_n,)),
-            dma((3 * ctx_n,)),
+            dma((ctx_n,)),
             dma((ctx_n,)),
             dma((ctx_n,)),
         ],

time: 152 us -> 140 us (0.921)
  Pallas kernels: 149 us -> 138 us
    pallas_call x1, Pallas kernels: 149 us -> 138 us  [fused_shards(): pl.pallas_call(mixer_kernel, out_shape=jax.ShapeDtypeStruct((ctx_n * own,...]
where the time goes in v3:
time: 140 us
  Pallas kernels  138 us (99%)
  local copies, waits for them, and re-layouts  1.87 us (1%)
    pallas_call x1, Pallas kernels, fused_shards(): pl.pallas_call(mixer_kernel, out_shape=jax.ShapeDtypeStruct((ctx_n * own,...  138 us

profile of v3, /device:TPU:28, one launch (start us, length us, event | category | flops | bytes accessed | tf_op | source)
XLA Modules:
  0.0 140.1 jit_solution(13080127601320882037)
XLA Ops:
  0.0 138.2 %mixer.1 = bf16[1024,256]{1,0:T(8,128)(2,1)} custom-call(bf16[256,1024]{1,0:T(8,128)(2,1)} %tokens.1, bf16[3,512,1024]{2,1,0:T(8,128)(2,1)} %weight.1, f32[3,3,1024]{2,1,0:T(4,128)} %taps.1, f32[1,128,2048]{2,1,0:T(8,128)} %filters_in.1, f32[1,128]{1,0:T(1,128)} %skip.1, bf16[1024,1024]{1,0:T(8,128)(2,1)} %constant.4.clone.forward_in, ...), custom_call_target="tpu_custom_call" | custom-call | flops 6442450944 | bytes 16777216 | tf_op jit(solution)/shard_map/mixer/pallas_call | solution.py:462
  138.2 1.9 %copy.9 = bf16[1024,256]{1,0:T(8,128)(2,1)} copy(bf16[1024,256]{1,0:T(8,128)(2,1)} %mixer.1) | data formatting | bytes 1048576

commit v4 on v3

--- a/solution.py
+++ b/solution.py
@@ -300,7 +300,7 @@
     proj[0:8, :] = jnp.zeros((8, 3 * own), jnp.float32)
 
     def project(at, ranks, begin, end):
-        row = 8 + at * rows if isinstance(at, int) else pl.multiple_of(8 + at * rows, 8)
+        row = pl.multiple_of(8 + at * rows, 8)
         total = None if begin else proj[pl.ds(row, rows), :]
         for r in ranks:
             q = rank(r)
@@ -332,19 +332,41 @@
     weights_from(z, (1 - y,))
     weights_from(rank(1), (y, 1 - y))
 
-    @pl.loop(0, NZ * NY)
-    def _(s):
-        @pl.when(s < NZ * NY - lead)
-        def _():
-            x_step(s + lead)
-
+    def place(s):
+        return rank(s // 2) * NY + (y + s) % 2
+
+    def complete(s):
         o, yy = rank(s // 2), (y + s) % 2
         arrived(block(o, yy, x, 1 - c))
         arrived(block(o, yy, 1 - x, 1 - c))
-        project(o * NY + yy, (0, 1), True, False)
+
+    early = NZ * NY - NY
+
+    @pl.loop(0, early)
+    def _(s):
+        @pl.when(s < NZ * NY - lead)
+        def _():
+            x_step(s + lead)
+
+        complete(s)
+        project(place(s), (0, 1), True, False)
+
+    weights_from(rank(3), (y, 1 - y))
+
+    @pl.loop(0, early)
+    def _(s):
+        project(place(s), (3,), False, False)
 
     weights_from(rank(2), (y, 1 - y))
-    weights_from(rank(3), (y, 1 - y))
+
+    @pl.loop(0, early)
+    def _(s):
+        project(place(s), (2,), False, True)
+
+    @pl.loop(early, NZ * NY)
+    def _(s):
+        complete(s)
+        project(place(s), (0, 1, 3, 2), True, True)
 
     tap = [
         [taps[p, t : t + 1, pl.ds(own_lane, own)] for t in range(3)] for p in range(3)
@@ -397,7 +419,6 @@
     for n in range(blocks):
         lanes = slice(n * own, (n + 1) * own)
         for half in range(per_tile):
-            project(n * per_tile + half, (2, 3), False, True)
             features(n * per_tile + half)
         signal[:, lanes] = jnp.dot(
             forward[:, tile:], wave[:, lanes], preferred_element_type=jnp.float32

time: 140 us -> 142 us (1.014)
  Pallas kernels: 138 us -> 140 us
    pallas_call x1, Pallas kernels: 138 us -> 140 us  [fused_shards(): pl.pallas_call(mixer_kernel, out_shape=jax.ShapeDtypeStruct((ctx_n * own,...]
where the time goes in v4:
time: 142 us
  Pallas kernels  140 us (99%)
  local copies, waits for them, and re-layouts  1.87 us (1%)
    pallas_call x1, Pallas kernels, fused_shards(): pl.pallas_call(mixer_kernel, out_shape=jax.ShapeDtypeStruct((ctx_n * own,...  140 us

profile of v4, /device:TPU:28, one launch (start us, length us, event | category | flops | bytes accessed | tf_op | source)
XLA Modules:
  0.0 141.5 jit_solution(7938592995319524411)
XLA Ops:
  0.0 139.6 %mixer.1 = bf16[1024,256]{1,0:T(8,128)(2,1)} custom-call(bf16[256,1024]{1,0:T(8,128)(2,1)} %tokens.1, bf16[3,512,1024]{2,1,0:T(8,128)(2,1)} %weight.1, f32[3,3,1024]{2,1,0:T(4,128)} %taps.1, f32[1,128,2048]{2,1,0:T(8,128)} %filters_in.1, f32[1,128]{1,0:T(1,128)} %skip.1, bf16[1024,1024]{1,0:T(8,128)(2,1)} %constant.4.clone.forward_in, ...), custom_call_target="tpu_custom_call" | custom-call | flops 6442450944 | bytes 16777216 | tf_op jit(solution)/shard_map/mixer/pallas_call | solution.py:483
  139.6 1.9 %copy.9 = bf16[1024,256]{1,0:T(8,128)(2,1)} copy(bf16[1024,256]{1,0:T(8,128)(2,1)} %mixer.1) | data formatting | bytes 1048576

commit v5 on v3

--- a/solution.py
+++ b/solution.py
@@ -169,31 +169,47 @@
     def block(zz, yy, xx, cc):
         return (zz * NY + yy) * (NX * NC) + xx * NC + cc
 
-    def push(b, sem, target):
+    half_rows = rows // 2
+    halves = (0, 1)
+
+    def part(b, h):
+        return tok.at[b, pl.ds(h * half_rows, half_rows)]
+
+    def push(b, h, sem, target):
         return pltpu.make_async_remote_copy(
-            src_ref=tok.at[b], dst_ref=tok.at[b], send_sem=sem, recv_sem=tok_recv.at[b],
+            src_ref=part(b, h), dst_ref=part(b, h), send_sem=sem, recv_sem=tok_recv.at[2 * b + h],
             device_id=target, device_id_type=MESH_ID,
         )
 
-    def up(o):
-        return push(block(o, y, x, c), z_send.at[o], device(z + 1, y, x, c))
-
-    def down(o):
-        return push(block(o, y, x, c), z_send.at[NZ + o], device(z - 1, y, x, c))
-
-    def to_y(o):
-        return push(block(o, y, x, c), y_send.at[o], device(z, 1 - y, x, c))
-
-    def to_x(o, yy):
-        return push(block(o, yy, x, c), x_send.at[o * NY + yy], device(z, y, 1 - x, c))
+    def up(o, h):
+        return push(block(o, y, x, c), h, z_send.at[2 * o + h], device(z + 1, y, x, c))
+
+    def down(o, h):
+        return push(
+            block(o, y, x, c), h, z_send.at[2 * (NZ + o) + h], device(z - 1, y, x, c)
+        )
+
+    def to_y(o, h):
+        return push(block(o, y, x, c), h, y_send.at[2 * o + h], device(z, 1 - y, x, c))
+
+    def to_x(o, yy, h):
+        return push(
+            block(o, yy, x, c), h, x_send.at[2 * (o * NY + yy) + h], device(z, y, 1 - x, c)
+        )
 
     def to_c(o, yy, xx):
-        return push(
-            block(o, yy, xx, c), c_send.at[(o * NY + yy) * NX + xx], device(z, y, x, 1 - c)
-        )
-
-    def arrived(b):
-        pltpu.make_async_copy(tok.at[b], tok.at[b], tok_recv.at[b]).wait()
+        b = block(o, yy, xx, c)
+        return pltpu.make_async_remote_copy(
+            src_ref=tok.at[b], dst_ref=tok.at[b],
+            send_sem=c_send.at[(o * NY + yy) * NX + xx], recv_sem=tok_recv.at[2 * b],
+            device_id=device(z, y, x, 1 - c), device_id_type=MESH_ID,
+        )
+
+    def arrived(b, h):
+        pltpu.make_async_copy(part(b, h), part(b, h), tok_recv.at[2 * b + h]).wait()
+
+    def arrived_whole(b):
+        pltpu.make_async_copy(tok.at[b], tok.at[b], tok_recv.at[2 * b]).wait()
 
     def rank(r):
         g = r // 2
@@ -223,16 +239,17 @@
     first.wait()
     pl.semaphore_wait(barrier, ctx_n + 1)
 
-    @pl.when(z < NZ - 1)
-    def _():
-        up(z).start()
-
-    @pl.when(z > 0)
-    def _():
-        down(z).start()
-
-    to_y(z).start()
-    to_x(z, y).start()
+    for h in halves:
+        @pl.when(z < NZ - 1)
+        def _():
+            up(z, h).start()
+
+        @pl.when(z > 0)
+        def _():
+            down(z, h).start()
+
+        to_y(z, h).start()
+        to_x(z, y, h).start()
     to_c(z, y, x).start()
 
     def weight_push(peer):
@@ -248,24 +265,26 @@
 
     def z_step(r):
         o = rank(r)
-        arrived(block(o, y, x, c))
-
-        @pl.when(jnp.logical_and(o < z, z < NZ - 1))
-        def _():
-            up(o).start()
-
-        @pl.when(jnp.logical_and(o > z, z > 0))
-        def _():
-            down(o).start()
-
-        to_y(o).start()
-        to_x(o, y).start()
+        for h in halves:
+            arrived(block(o, y, x, c), h)
+
+            @pl.when(jnp.logical_and(o < z, z < NZ - 1))
+            def _():
+                up(o, h).start()
+
+            @pl.when(jnp.logical_and(o > z, z > 0))
+            def _():
+                down(o, h).start()
+
+            to_y(o, h).start()
+            to_x(o, y, h).start()
         to_c(o, y, x).start()
 
     def y_step(r):
         o = rank(r)
-        arrived(block(o, 1 - y, x, c))
-        to_x(o, 1 - y).start()
+        for h in halves:
+            arrived(block(o, 1 - y, x, c), h)
+            to_x(o, 1 - y, h).start()
         to_c(o, 1 - y, x).start()
 
     for k, (src, dst) in enumerate(staged):
@@ -322,7 +341,8 @@
 
     def x_step(s):
         o, yy = rank(s // 2), (y + s) % 2
-        arrived(block(o, yy, 1 - x, c))
+        for h in halves:
+            arrived(block(o, yy, 1 - x, c), h)
         to_c(o, yy, 1 - x).start()
 
     lead = 4
@@ -339,8 +359,8 @@
             x_step(s + lead)
 
         o, yy = rank(s // 2), (y + s) % 2
-        arrived(block(o, yy, x, 1 - c))
-        arrived(block(o, yy, 1 - x, 1 - c))
+        arrived_whole(block(o, yy, x, 1 - c))
+        arrived_whole(block(o, yy, 1 - x, 1 - c))
         project(o * NY + yy, (0, 1), True, False)
 
     weights_from(rank(2), (y, 1 - y))
@@ -421,17 +441,19 @@
                 out_keep(q).start()
 
     for o in range(NZ):
-        @pl.when(jnp.logical_and(o <= z, z < NZ - 1))
-        def _():
-            up(o).wait_send()
-
-        @pl.when(jnp.logical_and(o >= z, z > 0))
-        def _():
-            down(o).wait_send()
-
-        to_y(o).wait_send()
+        for h in halves:
+            @pl.when(jnp.logical_and(o <= z, z < NZ - 1))
+            def _():
+                up(o, h).wait_send()
+
+            @pl.when(jnp.logical_and(o >= z, z > 0))
+            def _():
+                down(o, h).wait_send()
+
+            to_y(o, h).wait_send()
+            for yy in range(NY):
+                to_x(o, yy, h).wait_send()
         for yy in range(NY):
-            to_x(o, yy).wait_send()
             for xx in range(NX):
                 to_c(o, yy, xx).wait_send()
     for q in range(ctx_n):
@@ -479,10 +501,10 @@
             pltpu.VMEM((span, own), jnp.float32),
             pltpu.VMEM((ctx_n, own, rows), jnp.bfloat16),
             dma((6,)),
-            dma((ctx_n * ch_n,)),
+            dma((2 * ctx_n * ch_n,)),
+            dma((4 * NZ,)),
             dma((2 * NZ,)),
-            dma((NZ,)),
-            dma((ctx_n,)),
+            dma((2 * ctx_n,)),
             dma((ctx_n * NX,)),
             dma((ctx_n,)),
             dma((ctx_n,)),

time: 140 us -> 139 us (level)
    pallas_call x1, Pallas kernels: 138 us -> 137 us  [fused_shards(): pl.pallas_call(mixer_kernel, out_shape=jax.ShapeDtypeStruct((ctx_n * own,...]
where the time goes in v5:
time: 139 us; the launch traced here: 138 us
  Pallas kernels  137 us (99%)
  local copies, waits for them, and re-layouts  1.87 us (1%)
    pallas_call x1, Pallas kernels, fused_shards(): pl.pallas_call(mixer_kernel, out_shape=jax.ShapeDtypeStruct((ctx_n * own,...  137 us

profile of v5, /device:TPU:28, one launch (start us, length us, event | category | flops | bytes accessed | tf_op | source)
XLA Modules:
  0.0 138.4 jit_solution(8885652494074890231)
XLA Ops:
  0.0 136.5 %mixer.1 = bf16[1024,256]{1,0:T(8,128)(2,1)} custom-call(bf16[256,1024]{1,0:T(8,128)(2,1)} %tokens.1, bf16[3,512,1024]{2,1,0:T(8,128)(2,1)} %weight.1, f32[3,3,1024]{2,1,0:T(4,128)} %taps.1, f32[1,128,2048]{2,1,0:T(8,128)} %filters_in.1, f32[1,128]{1,0:T(1,128)} %skip.1, bf16[1024,1024]{1,0:T(8,128)(2,1)} %constant.4.clone.forward_in, ...), custom_call_target="tpu_custom_call" | custom-call | flops 6442450944 | bytes 16777216 | tf_op jit(solution)/shard_map/mixer/pallas_call | solution.py:484
  136.5 1.9 %copy.9 = bf16[1024,256]{1,0:T(8,128)(2,1)} copy(bf16[1024,256]{1,0:T(8,128)(2,1)} %mixer.1) | data formatting | bytes 1048576
